TPU v7x, 32 devices: a whole 2x2x4 slice. The times are simulated.
32 devices in a mesh: groups: 2 (over x), tok: 4 (over y, core), hid: 4 (over z).
Axes of the slice: x: 2, y: 2, z: 4, core: 2. Of those that a mesh axis runs over, the one named last changes fastest.
Arguments:
- tokens: bfloat16 [2048, 5376], P(('groups', 'tok'), 'hid'), parts along dimension 0, may hold values from -6 to 6
- w_query: bfloat16 [5376, 2048], P('tok', 'hid'), may hold values from -0.078125 to 0.078125
- key_weight: bfloat16 [5376, 1024], P('tok', 'hid'), may hold values from -0.078125 to 0.078125
- value_weight: bfloat16 [5376, 1024], P('tok', 'hid'), may hold values from -0.078125 to 0.078125
- w_out: bfloat16 [2048, 5376], P('tok', 'hid'), may hold values from -0.5 to 0.5
- query_norm_gain: float32 [128], replicated, may hold values from 0.5 to 2
- key_gain: float32 [128], replicated, may hold values from 0.5 to 2
- positions: int32 [2048], P('groups'), parts along dimension 0, may hold values from 0 to 131071, as said below
- grad_out: bfloat16 [2048, 5376], P(('groups', 'tok'), 'hid'), parts along dimension 0, may hold values from -6 to 6
Outputs:
- attn_out: bfloat16 [2048, 5376], P(('groups', 'tok'), 'hid'), parts along dimension 0
- grad_x: bfloat16 [2048, 5376], P(('groups', 'tok'), 'hid'), parts along dimension 0
- grad_wq: float32 [10752, 2048], P(('groups', 'tok'), 'hid'), parts along dimension 0
- key_weight_gradient: float32 [10752, 1024], P(('groups', 'tok'), 'hid'), parts along dimension 0
- value_weight_gradient: float32 [10752, 1024], P(('groups', 'tok'), 'hid'), parts along dimension 0
- grad_wo: float32 [4096, 5376], P(('groups', 'tok'), 'hid'), parts along dimension 0
There are 2 independent parts, one for each index of `groups`. A program takes and returns all parts, laid end to end along the dimension named above; an argument that names none is the same for every part. Nothing has to cross between parts.
Inputs may be any that keep to these rules, and one draw needn't show every extreme that they name: positions[t] is token t's position in its document: it rises by one from token to token and is 0 where a document begins; the first document begins before the window and its last token in the window has position 131071; at least one document begins inside the window.
All inputs are finite; a program needn't handle non-finite values.
Results may differ from a plain program's by a relative error of at most 0.02.
Values may be sent and summed in bfloat16 or wider, within the bound.
A program may use at most 192 MiB of HBM per device.

v0:
```python
import jax
import jax.numpy as jnp
from jax import lax
from jax.sharding import PartitionSpec as P

QUERY_HEADS = 16
KEY_VALUE_HEADS = 8
HEAD_SIZE = 128
WINDOW = 1024
TOK_DEV = 256
attn_scale = 168.0 ** (-0.5)
rope_base = 10000.0
norm_eps = 1e-06


def from_behind(value, axis, steps):
    count = lax.axis_size(axis)
    first, last = (max(0, -steps), min(count, count - steps))
    return lax.ppermute(value, axis, [(source, source + steps) for source in range(first, last)])


def rotary_tables(token_pos):
    half_dim = HEAD_SIZE // 2
    freqs = rope_base ** (-jnp.arange(half_dim, dtype=jnp.float32) * 2.0 / HEAD_SIZE)
    angles = token_pos.astype(jnp.float32)[:, None] * freqs[None, :]
    return (jnp.cos(angles), jnp.sin(angles))


def prepare_inputs(raw_values, gain_vector, cosine_table, sine_table):
    scaled = (
        raw_values
        * lax.rsqrt(jnp.mean(raw_values * raw_values, -1, keepdims=True) + norm_eps)
        * gain_vector
    )
    half_dim = scaled.shape[-1] // 2
    first_half = scaled[..., :half_dim]
    second_half = scaled[..., half_dim:]
    cos_rows = cosine_table[:, None, :]
    sin_rows = sine_table[:, None, :]
    return jnp.concatenate(
        [
            first_half * cos_rows - second_half * sin_rows,
            second_half * cos_rows + first_half * sin_rows,
        ],
        -1,
    )


def local(
    tokens, w_query, key_weight, value_weight, w_out, query_norm_gain, key_gain, positions, grad_out
):
    hidden_count = lax.axis_size("hid")
    block_index = lax.axis_index("tok")
    query_heads = QUERY_HEADS // hidden_count
    key_value_heads = KEY_VALUE_HEADS // hidden_count
    group_width = QUERY_HEADS // KEY_VALUE_HEADS
    reach = WINDOW // TOK_DEV
    span_rows = (reach + 1) * TOK_DEV
    leading_part = reach * TOK_DEV
    first_token = block_index * TOK_DEV
    query_cols = query_heads * HEAD_SIZE
    kv_cols = key_value_heads * HEAD_SIZE
    full_rows = lax.all_gather(tokens, "hid", axis=1, tiled=True)
    pieces = (
        lax.all_gather(w_query, "tok", axis=0, tiled=True),
        lax.all_gather(key_weight, "tok", axis=0, tiled=True),
        lax.all_gather(value_weight, "tok", axis=0, tiled=True),
    )
    columns = full_rows
    query_unnormed = jnp.dot(columns, pieces[0], preferred_element_type=jnp.float32)
    key_unnormed = jnp.dot(columns, pieces[1], preferred_element_type=jnp.float32)
    value_raw = jnp.dot(columns, pieces[2], preferred_element_type=jnp.float32)
    values_local = value_raw.astype(jnp.bfloat16)
    token_pos = lax.dynamic_slice_in_dim(positions, first_token, TOK_DEV, 0)
    cosine_table, sine_table = rotary_tables(token_pos)
    query_heads_raw = query_unnormed.reshape(TOK_DEV, query_heads, HEAD_SIZE)
    key_heads_raw = key_unnormed.reshape(TOK_DEV, key_value_heads, HEAD_SIZE)
    query_rows = (
        prepare_inputs(query_heads_raw, query_norm_gain, cosine_table, sine_table)
        .astype(jnp.bfloat16)
        .reshape(TOK_DEV, key_value_heads, group_width, HEAD_SIZE)
    )
    keys_local = prepare_inputs(key_heads_raw, key_gain, cosine_table, sine_table).astype(
        jnp.bfloat16
    )
    key_value = jnp.stack([keys_local.reshape(TOK_DEV, kv_cols), values_local], 0)
    blocks = [key_value]
    moving = key_value
    for turn_index in range(reach):
        moving = from_behind(moving, "tok", 1)
        blocks = [moving] + blocks
    window = jnp.concatenate(blocks, 1)
    key_window = window[0].reshape(span_rows, key_value_heads, HEAD_SIZE)
    value_window = window[1].reshape(span_rows, key_value_heads, HEAD_SIZE)
    query_index = first_token + jnp.arange(TOK_DEV, dtype=jnp.int32)
    key_index = first_token - leading_part + jnp.arange(span_rows, dtype=jnp.int32)
    padded_pos = jnp.pad(positions, (leading_part, 0))
    key_pos = lax.dynamic_slice_in_dim(padded_pos, first_token, span_rows, 0)
    distance = query_index[:, None] - key_index[None, :]
    allowed = (
        (key_index[None, :] >= 0)
        & (distance >= 0)
        & (distance < WINDOW)
        & (token_pos[:, None] - key_pos[None, :] == distance)
    )
    scores = (
        jnp.einsum("tkgd,ukd->kgtu", query_rows, key_window, preferred_element_type=jnp.float32)
        * attn_scale
    )
    weights = jnp.where(allowed[None, None], jnp.exp(scores), 0.0)
    probabilities = weights / jnp.sum(weights, -1, keepdims=True)
    rounded = probabilities.astype(jnp.bfloat16)
    attended = jnp.einsum(
        "kgtu,ukd->tkgd", rounded, value_window, preferred_element_type=jnp.float32
    )
    attended = attended.astype(jnp.bfloat16).reshape(TOK_DEV, query_cols)
    all_heads = lax.all_gather(attended, "hid", axis=1, tiled=True)
    columns = all_heads
    output = jnp.dot(
        columns,
        lax.all_gather(w_out, "tok", axis=0, tiled=True),
        preferred_element_type=jnp.float32,
    )
    attn_out = output.astype(jnp.bfloat16)
    partial_heads = jnp.einsum(
        "td,hd->th",
        grad_out,
        lax.all_gather(w_out, "tok", axis=0, tiled=True),
        preferred_element_type=jnp.float32,
    )
    attended_gradient = lax.psum_scatter(
        partial_heads.astype(jnp.bfloat16), "hid", scatter_dimension=1, tiled=True
    )
    attended_gradient = attended_gradient.reshape(TOK_DEV, key_value_heads, group_width, HEAD_SIZE)
    columns = all_heads
    grad_wo = lax.psum_scatter(
        jnp.einsum("th,td->hd", columns, grad_out, preferred_element_type=jnp.float32).astype(
            jnp.bfloat16
        ),
        "tok",
        scatter_dimension=0,
        tiled=True,
    ).astype(jnp.float32)
    grad_probs = jnp.einsum(
        "tkgd,ukd->kgtu", attended_gradient, value_window, preferred_element_type=jnp.float32
    )
    grad_scores = (
        attn_scale
        * probabilities
        * (grad_probs - jnp.sum(probabilities * grad_probs, -1, keepdims=True))
    )
    grad_scores = grad_scores.astype(jnp.bfloat16)
    grad_queries = jnp.einsum(
        "kgtu,ukd->tkgd", grad_scores, key_window, preferred_element_type=jnp.float32
    )
    keys_gradient = jnp.einsum(
        "kgtu,tkgd->ukd", grad_scores, query_rows, preferred_element_type=jnp.float32
    )
    values_gradient = jnp.einsum(
        "kgtu,tkgd->ukd", rounded, attended_gradient, preferred_element_type=jnp.float32
    )
    grad_window = jnp.stack(
        [keys_gradient.reshape(span_rows, kv_cols), values_gradient.reshape(span_rows, kv_cols)], 0
    )
    grad_kv = grad_window[:, :TOK_DEV]
    for turn_index in range(1, reach + 1):
        grad_kv = (
            from_behind(grad_kv.astype(jnp.bfloat16), "tok", -1).astype(grad_kv.dtype)
            + grad_window[:, turn_index * TOK_DEV : (turn_index + 1) * TOK_DEV]
        )
    _, query_pull = jax.vjp(
        lambda raw_values: prepare_inputs(raw_values, query_norm_gain, cosine_table, sine_table),
        query_heads_raw,
    )
    _, key_pullback = jax.vjp(
        lambda raw_values: prepare_inputs(raw_values, key_gain, cosine_table, sine_table),
        key_heads_raw,
    )
    query_back = (
        query_pull(grad_queries.reshape(TOK_DEV, query_heads, HEAD_SIZE))[0]
        .astype(jnp.bfloat16)
        .reshape(TOK_DEV, query_cols)
    )
    key_backward = (
        key_pullback(grad_kv[0].reshape(TOK_DEV, key_value_heads, HEAD_SIZE))[0]
        .astype(jnp.bfloat16)
        .reshape(TOK_DEV, kv_cols)
    )
    value_backward = grad_kv[1].astype(jnp.bfloat16)
    pieces = (
        lax.all_gather(w_query, "tok", axis=0, tiled=True),
        lax.all_gather(key_weight, "tok", axis=0, tiled=True),
        lax.all_gather(value_weight, "tok", axis=0, tiled=True),
    )
    block_rows = jnp.einsum("tc,dc->td", query_back, pieces[0], preferred_element_type=jnp.float32)
    block_rows = block_rows + jnp.einsum(
        "tc,dc->td", key_backward, pieces[1], preferred_element_type=jnp.float32
    )
    block_rows = block_rows + jnp.einsum(
        "tc,dc->td", value_backward, pieces[2], preferred_element_type=jnp.float32
    )
    grad_x = lax.psum_scatter(
        block_rows.astype(jnp.bfloat16), "hid", scatter_dimension=1, tiled=True
    )
    joined = jnp.concatenate([query_back, key_backward, value_backward], 1)
    columns = full_rows
    inputs_gradient = lax.psum_scatter(
        jnp.einsum("td,tc->dc", columns, joined, preferred_element_type=jnp.float32).astype(
            jnp.bfloat16
        ),
        "tok",
        scatter_dimension=0,
        tiled=True,
    ).astype(jnp.float32)
    grad_wq = inputs_gradient[:, :query_cols]
    key_weight_gradient = inputs_gradient[:, query_cols : query_cols + kv_cols]
    value_weight_gradient = inputs_gradient[:, query_cols + kv_cols :]
    return (attn_out, grad_x, grad_wq, key_weight_gradient, value_weight_gradient, grad_wo)


def solution(mesh):
    return jax.shard_map(
        local,
        mesh=mesh,
        in_specs=(
            P(("groups", "tok"), "hid"),
            P("tok", "hid"),
            P("tok", "hid"),
            P("tok", "hid"),
            P("tok", "hid"),
            P(),
            P(),
            P("groups"),
            P(("groups", "tok"), "hid"),
        ),
        out_specs=(
            P(("groups", "tok"), "hid"),
            P(("groups", "tok"), "hid"),
            P(("groups", "tok"), "hid"),
            P(("groups", "tok"), "hid"),
            P(("groups", "tok"), "hid"),
            P(("groups", "tok"), "hid"),
        ),
        check_vma=False,
    )
```

profile of v0, /device:TPU:0, one launch (start us, length us, event | category | flops | bytes accessed | tf_op | source)
XLA Modules:
  0.0 533.1 jit_solution(8596791121754949615)
XLA Ops:
  12.1 57.2 %all-gather.7.cloned.1.call-done = bf16[256,5376]{0,1:T(8,128)(2,1)} async-done(((bf16[256,1344]{0,1:T(8,128)(2,1)}), bf16[256,5376]{0,1:T(8,128)(2,1)}) %all-gather.7.cloned.1.call-update) | async-done | bytes 2752528 | tf_op jit(solution)/shard_map/all_gather | solution.py:63
  69.3 26.6 %all-gather.9.cloned.1.call-done = bf16[5376,256]{1,0:T(8,128)(2,1)} async-done(((bf16[1344,256]{1,0:T(8,128)(2,1)}), bf16[5376,256]{1,0:T(8,128)(2,1)}) %all-gather.9.cloned.1.call-update) | async-done | bytes 2752528 | tf_op jit(solution)/shard_map/all_gather | solution.py:66
  95.9 3.8 multiply_reduce_fusion.3
  103.0 20.9 %all-gather.11.cloned.1.call-done = bf16[5376,256]{1,0:T(8,128)(2,1)} async-done(((bf16[1344,256]{1,0:T(8,128)(2,1)}), bf16[5376,256]{1,0:T(8,128)(2,1)}) %all-gather.11.cloned.1.call-update) | async-done | bytes 2752528 | tf_op jit(solution)/shard_map/all_gather | solution.py:67
  123.9 2.7 fusion.17
  127.3 2.1 collective-permute-start
  131.3 4.9 collective-permute-start.1
  137.0 12.5 %collective-permute-start.2 = (bf16[2,256,256]{2,1,0:T(8,128)(2,1)}, bf16[2,256,256]{2,1,0:T(8,128)(2,1)}, u32[]{:S(2)}, u32[]{:S(2)}) collective-permute-start(bf16[2,256,256]{2,1,0:T(8,128)(2,1)} %collective-permute-done.1), channel_id=1, source_target_pairs={{0,4},{4,8},{8,12},{1,5},{5,9},{9,13},{2,6},{6,10},{10,14},{3,7},{... | collective-permute-start | bytes 786440 | tf_op jit(solution)/shard_map/ppermute | solution.py:19
  150.3 12.2 %collective-permute-start.3 = (bf16[2,256,256]{2,1,0:T(8,128)(2,1)}, bf16[2,256,256]{2,1,0:T(8,128)(2,1)S(1)}, u32[]{:S(2)}, u32[]{:S(2)}) collective-permute-start(bf16[2,256,256]{2,1,0:T(8,128)(2,1)} %collective-permute-done.2), channel_id=1, source_target_pairs={{0,4},{4,8},{8,12},{1,5},{5,9},{9,13},{2,6},{6,10},{10,14},{3,7},{... | collective-permute-start | bytes 786440 | tf_op jit(solution)/shard_map/ppermute | solution.py:19
  162.5 2.1 fusion.11
  165.3 1.7 constant_dynamic-update-slice_fusion.3
  167.0 1.7 constant_dynamic-update-slice_fusion.2
  170.9 5.3 %convolution_convert_fusion.3 = bf16[256,2048]{1,0:T(8,128)(2,1)} fusion(bf16[256,1344]{0,1:T(8,128)(2,1)S(1)} %copy-done, bf16[2048,1344]{0,1:T(8,128)(2,1)} %all-gather.17.cloned.1.call-done), kind=kOutput, calls=%fused_computation.23 | convolution fusion | flops 1409810432 | bytes 7241728 | tf_op jit(solution)/shard_map/td,hd->th/dot_general | solution.py:125
  176.5 1.7 constant_dynamic-update-slice_fusion
  178.2 2.4 fusion.50
  180.6 2.5 reshape_squeeze.9
  183.2 2.6 reshape_squeeze.10
  185.7 3.0 copy.117
  188.7 29.4 %all-gather.13.cloned.1.call-done = bf16[5376,512]{1,0:T(8,128)(2,1)} async-done(((bf16[1344,512]{1,0:T(8,128)(2,1)}), bf16[5376,512]{1,0:T(8,128)(2,1)}) %all-gather.13.cloned.1.call-update) | async-done | bytes 5505040 | tf_op jit(solution)/shard_map/all_gather | solution.py:65
  218.1 5.0 fusion.53
  225.9 22.1 %reduce-scatter.7.cloned.1.call-done = bf16[256,512]{1,0:T(8,128)(2,1)} async-done(((bf16[256,2048]{1,0:T(8,128)(2,1)}), bf16[256,512]{1,0:T(8,128)(2,1)}) %reduce-scatter.7.cloned.1.call-update) | async-done | bytes 262160 | tf_op jit(solution)/shard_map/reduce_scatter | solution.py:131
  249.1 3.2 fusion.19
  252.3 7.2 %fusion.2 = (f32[2,2,256]{2,1,0:T(2,128)S(1)}, f32[2,2,256,1280]{2,3,1,0:T(8,128)}) fusion(f32[2,1280,256,2]{2,1,3,0:T(8,128)} %fusion.19, bf16[1280,2,128,1]{0,2,3,1:T(8,128)(2,1)S(1)} %copy-done.14, pred[256,1280]{0,1:T(8,128)(4,1)S(1)} %copy-done.34, bf16[256,2,2,64]{3,0,2,1:T(8,128)(2,1)S(1)} %bitcast.103, bf16[256,2,2,64]{3,0,2,1:T(8,128)(2,1)S(1)} %bitcast.105), kind=kOutput, calls=%fused_computation.8 | convolution fusion | flops 342623488 | bytes 11735040 | tf_op jit(solution)/shard_map/div | solution.py:111
  259.5 3.8 fusion.14
  263.3 26.7 %all-gather.15.cloned.1.call-done = bf16[256,2048]{0,1:T(8,128)(2,1)} async-done(((bf16[256,512]{0,1:T(8,128)(2,1)}), bf16[256,2048]{0,1:T(8,128)(2,1)}) %all-gather.15.cloned.1.call-update) | async-done | bytes 1048592 | tf_op jit(solution)/shard_map/all_gather | solution.py:117
  290.0 5.2 convolution_convert_fusion.1
  295.5 4.8 fusion.4
  301.4 4.5 fusion.7
  307.5 2.1 collective-permute-done.4
  314.2 3.2 collective-permute-done.5
  317.4 1.7 fusion.32
  322.5 10.5 %collective-permute-done.6 = bf16[2,256,256]{1,2,0:T(8,128)(2,1)} collective-permute-done((bf16[2,256,256]{1,2,0:T(8,128)(2,1)}, bf16[2,256,256]{1,2,0:T(8,128)(2,1)}, u32[]{:S(2)}, u32[]{:S(2)}) %collective-permute-start.6) | collective-permute-done | bytes 262176 | tf_op jit(solution)/shard_map/ppermute | solution.py:19
  333.0 1.7 fusion.24
  336.2 2.0 fusion.21
  339.0 9.6 %collective-permute-done.7 = bf16[2,256,256]{1,2,0:T(8,128)(2,1)} collective-permute-done((bf16[2,256,256]{1,2,0:T(8,128)(2,1)}, bf16[2,256,256]{1,2,0:T(8,128)(2,1)}, u32[]{:S(2)}, u32[]{:S(2)}) %collective-permute-start.7) | collective-permute-done | bytes 262176 | tf_op jit(solution)/shard_map/ppermute | solution.py:19
  352.2 7.7 %fusion = bf16[5376,1024]{0,1:T(8,128)(2,1)} fusion(bf16[256,5376]{0,1:T(8,128)(2,1)} %all-gather.7.cloned.1.call-done, bf16[256,256]{1,0:T(8,128)(2,1)S(1)} %copy.109, bf16[256,256]{1,0:T(8,128)(2,1)S(1)} %copy.108, bf16[256,512]{1,0:T(8,128)(2,1)S(1)} %bitcast.102), kind=kOutput, calls=%fused_computation.1 | convolution fusion | flops 2825650176 | bytes 14286848 | tf_op jit(solution)/shard_map/td,tc->dc/dot_general | solution.py:208
  359.9 14.7 %copy.133 = bf16[5376,1024]{1,0:T(8,128)(2,1)} copy(bf16[5376,1024]{0,1:T(8,128)(2,1)} %fusion) | data formatting | bytes 22020096
  375.5 4.3 fusion.47
  381.7 2.5 fusion.1
  385.5 5.5 %convolution_convert_fusion.2 = bf16[256,1344]{0,1:T(8,128)(2,1)} fusion(bf16[2048,1344]{0,1:T(8,128)(2,1)} %all-gather.17.cloned.1.call-done, bf16[256,2048]{0,1:T(8,128)(2,1)S(1)} %copy-done.26), kind=kOutput, calls=%fused_computation.22 | convolution fusion | flops 1409630208 | bytes 7241728 | tf_op jit(solution)/shard_map/dot_general | solution.py:119
  391.0 3.6 convert_element_type.111
  394.6 74.7 %reduce-scatter.13.cloned.1.call-done = bf16[1344,1024]{1,0:T(8,128)(2,1)} async-done(((bf16[5376,1024]{1,0:T(8,128)(2,1)}), bf16[1344,1024]{1,0:T(8,128)(2,1)}) %reduce-scatter.13.cloned.1.call-update) | async-done | bytes 2752528
  469.3 4.6 copy.134
  473.9 3.1 slice.82
  477.0 3.8 copy.110
  480.8 2.6 fusion.49
  483.4 2.9 copy.111
  487.8 38.4 %reduce-scatter.9.cloned.1.call-done = bf16[256,1344]{0,1:T(8,128)(2,1)} async-done(((bf16[256,5376]{0,1:T(8,128)(2,1)}), bf16[256,1344]{0,1:T(8,128)(2,1)}) %reduce-scatter.9.cloned.1.call-update) | async-done | bytes 688144 | tf_op jit(solution)/shard_map/reduce_scatter | solution.py:202
  (157 shorter events, 41.0 us)
Async XLA Ops:
  7.2 163.8 %copy-start = (bf16[256,1344]{0,1:T(8,128)(2,1)S(1)}, bf16[256,1344]{0,1:T(8,128)(2,1)}, u32[]{:S(2)}) copy-start(bf16[256,1344]{0,1:T(8,128)(2,1)} %param.17) | copy-start | bytes 2064388
  7.2 3.5 copy-start.36
  7.2 62.1 %all-gather.7.cloned.1.call-start = ((), (), s32[]{:S(2)}) async-start(), calls=%async_computation.4 | async-start | bytes 3440640 | tf_op jit(solution)/shard_map/all_gather | solution.py:63
  7.9 88.0 %all-gather.9.cloned.1.call-start = ((), (), s32[]{:S(2)}) async-start(), calls=%async_computation.5 | async-start | bytes 3440640 | tf_op jit(solution)/shard_map/all_gather | solution.py:66
  8.7 115.2 %all-gather.11.cloned.1.call-start = ((), (), s32[]{:S(2)}) async-start(), calls=%async_computation.6 | async-start | bytes 3440640 | tf_op jit(solution)/shard_map/all_gather | solution.py:67
  9.4 161.5 %all-gather.17.cloned.1.call-start = ((), (), s32[]{:S(2)}) async-start(), calls=%async_computation.9 | async-start | bytes 6881280 | tf_op jit(solution)/shard_map/all_gather | solution.py:121
  10.0 208.1 %all-gather.13.cloned.1.call-start = ((), (), s32[]{:S(2)}) async-start(), calls=%async_computation.7 | async-start | bytes 6881280 | tf_op jit(solution)/shard_map/all_gather | solution.py:65
  10.6 237.4 %reduce-scatter.7.cloned.1.call-start = ((), (), s32[]{:S(2)}) async-start(), calls=%async_computation.10 | async-start | bytes 1310720 | tf_op jit(solution)/shard_map/reduce_scatter | solution.py:131
  12.1 88.4 %copy-start.38 = (f32[128]{0:T(128)S(1)}, f32[128]{0:T(128)}, u32[]{:S(2)}) copy-start(f32[128]{0:T(128)} %param.15) | copy-start | bytes 1540
  69.3 54.6 %copy-start.2 = (bf16[256,5376]{0,1:T(8,128)(2,1)S(1)}, bf16[256,5376]{0,1:T(8,128)(2,1)}, u32[]{:S(2)}) copy-start(bf16[256,5376]{0,1:T(8,128)(2,1)} %all-gather.7.cloned.1.call-done) | copy-start | bytes 8257540
  95.9 4.6 copy-start.31
  123.9 2.8 copy-start.29
  127.3 3.3 collective-permute-start
  131.3 5.8 %collective-permute-start.1 = (bf16[2,256,256]{2,1,0:T(8,128)(2,1)S(1)}, bf16[2,256,256]{2,1,0:T(8,128)(2,1)}, u32[]{:S(2)}, u32[]{:S(2)}) collective-permute-start(bf16[2,256,256]{2,1,0:T(8,128)(2,1)S(1)} %collective-permute-done), channel_id=1, source_target_pairs={{0,4},{4,8},{8,12},{1,5},{5,9},{9,13},{2,6},{6,10},{10,14},{3,7},{... | collective-permute-start | bytes 786440 | tf_op jit(solution)/shard_map/ppermute | solution.py:19
  137.0 13.2 %collective-permute-start.2 = (bf16[2,256,256]{2,1,0:T(8,128)(2,1)}, bf16[2,256,256]{2,1,0:T(8,128)(2,1)}, u32[]{:S(2)}, u32[]{:S(2)}) collective-permute-start(bf16[2,256,256]{2,1,0:T(8,128)(2,1)} %collective-permute-done.1), channel_id=1, source_target_pairs={{0,4},{4,8},{8,12},{1,5},{5,9},{9,13},{2,6},{6,10},{10,14},{3,7},{... | collective-permute-start | bytes 786440 | tf_op jit(solution)/shard_map/ppermute | solution.py:19
  150.3 14.3 %collective-permute-start.3 = (bf16[2,256,256]{2,1,0:T(8,128)(2,1)}, bf16[2,256,256]{2,1,0:T(8,128)(2,1)S(1)}, u32[]{:S(2)}, u32[]{:S(2)}) collective-permute-start(bf16[2,256,256]{2,1,0:T(8,128)(2,1)} %collective-permute-done.2), channel_id=1, source_target_pairs={{0,4},{4,8},{8,12},{1,5},{5,9},{9,13},{2,6},{6,10},{10,14},{3,7},{... | collective-permute-start | bytes 786440 | tf_op jit(solution)/shard_map/ppermute | solution.py:19
  176.3 113.7 %all-gather.15.cloned.1.call-start = ((), (), s32[]{:S(2)}) async-start(), calls=%async_computation.8 | async-start | bytes 1310720 | tf_op jit(solution)/shard_map/all_gather | solution.py:117
  188.7 36.2 %copy-start.37 = (f32[128]{0:T(128)S(1)}, f32[128]{0:T(128)}, u32[]{:S(2)}) copy-start(f32[128]{0:T(128)} %param.14) | copy-start | bytes 1540
  223.0 2.2 copy-start.20
  223.0 2.2 copy-start.22
  224.3 24.8 %copy-start.3 = (f32[256,4,128]{2,1,0:T(4,128)}, f32[256,4,128]{2,1,0:T(4,128)S(1)}, u32[]{:S(2)}) copy-start(f32[256,4,128]{2,1,0:T(4,128)S(1)} %reshape.224) | copy-start | bytes 1572868
  224.3 24.8 %copy-start.6 = (bf16[1280,2,128]{2,1,0:T(2,128)(2,1)S(1)}, bf16[1280,2,128]{2,1,0:T(2,128)(2,1)}, u32[]{:S(2)}) copy-start(bf16[1280,2,128]{2,1,0:T(2,128)(2,1)} %reshape_squeeze.9) | copy-start | bytes 1966084
  224.9 24.2 %copy-start.27 = (f32[256,4]{1,0:T(8,128)}, f32[256,4]{1,0:T(8,128)S(1)}, u32[]{:S(2)}) copy-start(f32[256,4]{1,0:T(8,128)S(1)} %copy.90) | copy-start | bytes 12292
  249.1 3.2 copy-start.17
  249.1 3.2 copy-start.14
  249.1 3.2 copy-start.34
  263.3 127.7 %reduce-scatter.11.cloned.1.call-start = ((), (), s32[]{:S(2)}) async-start(), calls=%async_computation.12 | async-start | bytes 6881280 | tf_op jit(solution)/shard_map/reduce_scatter | solution.py:136
  295.3 174.0 %reduce-scatter.13.cloned.1.call-start = ((), (), s32[]{:S(2)}) async-start(), calls=%async_computation.13 | async-start | bytes 13762560
  306.0 5.7 %copy-start.15 = (bf16[1280,2,128,1]{0,2,3,1:T(8,128)(2,1)S(1)}, bf16[1280,2,128,1]{0,2,3,1:T(8,128)(2,1)}, u32[]{:S(2)}) copy-start(bf16[1280,2,128,1]{0,2,3,1:T(8,128)(2,1)} %copy.117) | copy-start | bytes 1966084
  306.0 3.6 collective-permute-start.4
  310.4 7.1 %collective-permute-start.5 = (bf16[2,256,256]{1,2,0:T(8,128)(2,1)}, bf16[2,256,256]{1,2,0:T(8,128)(2,1)}, u32[]{:S(2)}, u32[]{:S(2)}) collective-permute-start(bf16[2,256,256]{1,2,0:T(8,128)(2,1)} %fusion.29), channel_id=1, source_target_pairs={{4,0},{8,4},{12,8},{5,1},{9,5},{13,9},{6,2},{10,6},{14,10},{7,3},{... | collective-permute-start | bytes 786440 | tf_op jit(solution)/shard_map/ppermute | solution.py:19
  312.2 8.3 %copy-start.23 = (f32[256,64]{1,0:T(8,128)S(1)}, f32[256,64]{1,0:T(8,128)}, u32[]{:S(2)}) copy-start(f32[256,64]{1,0:T(8,128)} %copy-done.21) | copy-start | bytes 196612
  314.2 6.2 %copy-start.24 = (f32[256,4,64]{2,1,0:T(4,128)S(1)}, f32[256,4,64]{2,1,0:T(4,128)}, u32[]{:S(2)}) copy-start(f32[256,4,64]{2,1,0:T(4,128)} %copy.136) | copy-start | bytes 786436
  314.2 6.2 %copy-start.25 = (f32[256,4,64]{2,1,0:T(4,128)S(1)}, f32[256,4,64]{2,1,0:T(4,128)}, u32[]{:S(2)}) copy-start(f32[256,4,64]{2,1,0:T(4,128)} %copy.135) | copy-start | bytes 786436
  314.2 7.5 %copy-start.4 = (f32[256,4,128]{2,1,0:T(4,128)S(1)}, f32[256,4,128]{2,1,0:T(4,128)}, u32[]{:S(2)}) copy-start(f32[256,4,128]{2,1,0:T(4,128)} %copy-done.3) | copy-start | bytes 1572868
  319.1 13.9 %collective-permute-start.6 = (bf16[2,256,256]{1,2,0:T(8,128)(2,1)}, bf16[2,256,256]{1,2,0:T(8,128)(2,1)}, u32[]{:S(2)}, u32[]{:S(2)}) collective-permute-start(bf16[2,256,256]{1,2,0:T(8,128)(2,1)} %fusion.32), channel_id=1, source_target_pairs={{4,0},{8,4},{12,8},{5,1},{9,5},{13,9},{6,2},{10,6},{14,10},{7,3},{... | collective-permute-start | bytes 786440 | tf_op jit(solution)/shard_map/ppermute | solution.py:19
  320.8 15.4 %copy-start.28 = (f32[256,4]{1,0:T(8,128)S(1)}, f32[256,4]{1,0:T(8,128)}, u32[]{:S(2)}) copy-start(f32[256,4]{1,0:T(8,128)} %copy-done.27) | copy-start | bytes 12292
  334.7 13.9 %collective-permute-start.7 = (bf16[2,256,256]{1,2,0:T(8,128)(2,1)}, bf16[2,256,256]{1,2,0:T(8,128)(2,1)}, u32[]{:S(2)}, u32[]{:S(2)}) collective-permute-start(bf16[2,256,256]{1,2,0:T(8,128)(2,1)} %fusion.24), channel_id=1, source_target_pairs={{4,0},{8,4},{12,8},{5,1},{9,5},{13,9},{6,2},{10,6},{14,10},{7,3},{... | collective-permute-start | bytes 786440 | tf_op jit(solution)/shard_map/ppermute | solution.py:19
  338.2 11.4 %copy-start.9 = (bf16[256,4,128]{2,1,0:T(4,128)(2,1)}, bf16[256,4,128]{2,1,0:T(4,128)(2,1)S(1)}, u32[]{:S(2)}) copy-start(bf16[256,4,128]{2,1,0:T(4,128)(2,1)S(1)} %fusion.21) | copy-start | bytes 786436
  338.2 11.6 %copy-start.32 = (f32[256,64]{0,1:T(8,128)S(1)}, f32[256,64]{0,1:T(8,128)}, u32[]{:S(2)}) copy-start(f32[256,64]{0,1:T(8,128)} %copy.86) | copy-start | bytes 196612
  349.6 10.2 %copy-start.12 = (f32[2,256,256]{1,2,0:T(8,128)}, f32[2,256,256]{1,2,0:T(8,128)S(1)}, u32[]{:S(2)}) copy-start(f32[2,256,256]{1,2,0:T(8,128)S(1)} %fusion.33) | copy-start | bytes 1572868
  349.6 2.5 copy-start.30
  374.6 151.6 %reduce-scatter.9.cloned.1.call-start = ((), (), s32[]{:S(2)}) async-start(), calls=%async_computation.11 | async-start | bytes 3440640 | tf_op jit(solution)/shard_map/reduce_scatter | solution.py:202
  375.5 4.4 copy-start.5
  379.9 1.8 copy-start.11
  379.9 1.9 copy-start.13
  384.3 1.2 copy-start.26
  483.4 42.8 %copy-start.1 = (bf16[256,1344]{0,1:T(8,128)(2,1)S(1)}, bf16[256,1344]{0,1:T(8,128)(2,1)}, u32[]{:S(2)}) copy-start(bf16[256,1344]{0,1:T(8,128)(2,1)} %param.17) | copy-start | bytes 2064388
  (9 other events, 7.4 us)
Sparse Core Ops, SparseCore 0:
  9.6 59.6 all-gather.6
  70.9 25.0 all-gather.8
  97.5 26.3 all-gather.10
  125.3 45.5 all-gather.16
  172.3 45.6 all-gather.12
  220.8 27.1 reduce-scatter.6
  263.4 26.5 all-gather.14
  295.4 59.1 reduce-scatter.10
  374.7 94.5 reduce-scatter.12
  472.1 54.1 reduce-scatter.8
where the time goes:
time: 535 us; the launch traced here: 533 us
  waiting for transfers between devices  328 us (61%)
  local copies, waits for them, and re-layouts  63.6 us (12%)
  matrix products  63.2 us (12%)
  starting transfers between devices  38.1 us (7%)
  other arithmetic  25.4 us (5%)
  between operations  14.9 us (3%)
    unnamed x11, waiting for transfers between devices  77.9 us
    all_gather x1, waiting for transfers between devices, local(): full_rows = lax.all_gather(tokens, 'hid', axis=1, tiled=True)  57.2 us
    unnamed x90, local copies, waits for them, and re-layouts  41.8 us
    reduce_scatter x1, waiting for transfers between devices, local(): lax.psum_scatter(block_rows.astype(jnp.bfloat16), 'hid', scatter_dimensio...  38.4 us
    ppermute x8, starting transfers between devices, from_behind(): lax.ppermute(value, axis, [(source, source + steps) for source in range(f...  37 us
    all_gather x1, waiting for transfers between devices, local(): lax.all_gather(w_query, 'tok', axis=0, tiled=True)  29.4 us
    ppermute x8, waiting for transfers between devices, from_behind(): lax.ppermute(value, axis, [(source, source + steps) for source in range(f...  28.1 us
    all_gather x1, waiting for transfers between devices, local(): all_heads = lax.all_gather(attended, 'hid', axis=1, tiled=True)  26.7 us
  transfers between devices with their start and end apart: 18, of which 16 were waited for; matrix products, arithmetic and copies ran while one was open for 24% of the time, Pallas kernels for 0%

commit v1 on v0

--- a/solution.py
+++ b/solution.py
@@ -11,6 +11,28 @@
 attn_scale = 168.0 ** (-0.5)
 rope_base = 10000.0
 norm_eps = 1e-06
+
+
+def in_order(blocks, dim):
+    lengths = list(blocks.shape[1:])
+    lengths[dim] *= blocks.shape[0]
+    return jnp.moveaxis(blocks, 0, dim).reshape(lengths)
+
+
+def collect(x, axis, dim):
+    peers = lax.axis_size(axis)
+    pairs = [(i, (i + 1) % peers) for i in range(peers)]
+    back = [(b, a) for a, b in pairs]
+    lower, upper = ([], [])
+    for lap in range(peers - 1):
+        if lap % 2 == 0:
+            lower.append(lax.ppermute(lower[-1] if lower else x, axis, pairs))
+        else:
+            upper.append(lax.ppermute(upper[-1] if upper else x, axis, back))
+    blocks = jnp.stack([*lower[::-1], x, *upper])
+    shift = lax.axis_index(axis) - len(lower)
+    blocks = blocks[(jnp.arange(peers) - shift) % peers]
+    return in_order(blocks, dim)
 
 
 def from_behind(value, axis, steps):
@@ -64,7 +86,7 @@
     pieces = (
         lax.all_gather(w_query, "tok", axis=0, tiled=True),
         lax.all_gather(key_weight, "tok", axis=0, tiled=True),
-        lax.all_gather(value_weight, "tok", axis=0, tiled=True),
+        collect(value_weight, "tok", 0),
     )
     columns = full_rows
     query_unnormed = jnp.dot(columns, pieces[0], preferred_element_type=jnp.float32)

time: 535 us -> 507 us (0.948)
  waiting for transfers between devices: 328 us -> 280 us
  starting transfers between devices: 38.1 us -> 47.5 us
  matrix products: 63.2 us -> 69.4 us
    all_gather x1, waiting for transfers between devices: 57.2 us -> 28.8 us  [local(): full_rows = lax.all_gather(tokens, 'hid', axis=1, tiled=True)]
    all_gather x1, waiting for transfers between devices: 20.9 us -> 0.01 us  [local(): lax.all_gather(value_weight, 'tok', axis=0, tiled=True)]
    ppermute x0 -> x3, waiting for transfers between devices: none -> 19.7 us  [the longest x2 19.7 us: collect(): lower.append(lax.ppermute(lower[-1] if lower else x, axis, pairs))]
    all_gather x1, waiting for transfers between devices: 29.4 us -> 18.4 us  [local(): lax.all_gather(w_query, 'tok', axis=0, tiled=True)]
    ppermute x8, waiting for transfers between devices: 28.1 us -> 21.8 us  [from_behind(): lax.ppermute(value, axis, [(source, source + steps) for source in range(f...]
    unnamed x90 -> x94, local copies, waits for them, and re-layouts: 41.8 us -> 40.8 us
  transfers between devices with their start and end apart: 18 -> 21, of which waited for: 16 -> 16; matrix products, arithmetic and copies ran while one was open for 24% -> 28% of each run, Pallas kernels for 0% -> 0%
where the time goes in v1:
time: 507 us; the launch traced here: 505 us
  waiting for transfers between devices  280 us (55%)
  matrix products  69.4 us (14%)
  local copies, waits for them, and re-layouts  64.8 us (13%)
  starting transfers between devices  47.5 us (9%)
  other arithmetic  28.4 us (6%)
  between operations  14.9 us (3%)
    unnamed x11, waiting for transfers between devices  78.1 us
    ppermute x8, starting transfers between devices, from_behind(): lax.ppermute(value, axis, [(source, source + steps) for source in range(f...  41.4 us
    unnamed x94, local copies, waits for them, and re-layouts  40.8 us
    reduce_scatter x1, waiting for transfers between devices, local(): lax.psum_scatter(block_rows.astype(jnp.bfloat16), 'hid', scatter_dimensio...  38.4 us
    all_gather x1, waiting for transfers between devices, local(): full_rows = lax.all_gather(tokens, 'hid', axis=1, tiled=True)  28.8 us
    all_gather x1, waiting for transfers between devices, local(): lax.all_gather(key_weight, 'tok', axis=0, tiled=True)  26.6 us
    all_gather x1, waiting for transfers between devices, local(): all_heads = lax.all_gather(attended, 'hid', axis=1, tiled=True)  25.9 us
    reduce_scatter x1, waiting for transfers between devices, local(): lax.psum_scatter(partial_heads.astype(jnp.bfloat16), 'hid', scatter_dimen...  22.1 us
  transfers between devices with their start and end apart: 21, of which 16 were waited for; matrix products, arithmetic and copies ran while one was open for 28% of the time, Pallas kernels for 0%

profile of v1, /device:TPU:0, one launch (start us, length us, event | category | flops | bytes accessed | tf_op | source)
XLA Modules:
  0.0 504.9 jit_solution(663102702426551453)
XLA Ops:
  10.6 2.0 collective-permute-start.2
  12.6 13.3 %collective-permute-done = bf16[1344,256]{1,0:T(8,128)(2,1)S(1)} collective-permute-done((bf16[1344,256]{1,0:T(8,128)(2,1)S(1)}, bf16[1344,256]{1,0:T(8,128)(2,1)S(1)}, u32[]{:S(2)}, u32[]{:S(2)}) %collective-permute-start) | collective-permute-done | bytes 688160 | tf_op jit(solution)/shard_map/ppermute | solution.py:29
  25.8 2.5 collective-permute-start.1
  29.9 6.5 %collective-permute-done.1 = bf16[1344,256]{1,0:T(8,128)(2,1)} collective-permute-done((bf16[1344,256]{1,0:T(8,128)(2,1)S(1)}, bf16[1344,256]{1,0:T(8,128)(2,1)}, u32[]{:S(2)}, u32[]{:S(2)}) %collective-permute-start.1) | collective-permute-done | bytes 688160 | tf_op jit(solution)/shard_map/ppermute | solution.py:29
  38.3 2.3 gather_fusion
  40.5 28.8 %all-gather.7.cloned.1.call-done = bf16[256,5376]{0,1:T(8,128)(2,1)} async-done(((bf16[256,1344]{0,1:T(8,128)(2,1)}), bf16[256,5376]{0,1:T(8,128)(2,1)}) %all-gather.7.cloned.1.call-update) | async-done | bytes 2752528 | tf_op jit(solution)/shard_map/all_gather | solution.py:85
  69.3 26.6 %all-gather.9.cloned.1.call-done = bf16[5376,256]{1,0:T(8,128)(2,1)} async-done(((bf16[1344,256]{1,0:T(8,128)(2,1)}), bf16[5376,256]{1,0:T(8,128)(2,1)}) %all-gather.9.cloned.1.call-update) | async-done | bytes 2752528 | tf_op jit(solution)/shard_map/all_gather | solution.py:88
  96.0 3.8 multiply_reduce_fusion.3
  103.0 3.3 fusion.17
  106.9 2.1 collective-permute-start.3
  110.9 10.4 %collective-permute-start.4 = (bf16[2,256,256]{2,1,0:T(8,128)(2,1)S(1)}, bf16[2,256,256]{2,1,0:T(8,128)(2,1)}, u32[]{:S(2)}, u32[]{:S(2)}) collective-permute-start(bf16[2,256,256]{2,1,0:T(8,128)(2,1)S(1)} %collective-permute-done.3), channel_id=1, source_target_pairs={{0,4},{4,8},{8,12},{1,5},{5,9},{9,13},{2,6},{6,10},{10,14},{3,7},{... | collective-permute-start | bytes 786440 | tf_op jit(solution)/shard_map/ppermute | solution.py:41
  121.8 12.7 %collective-permute-start.5 = (bf16[2,256,256]{2,1,0:T(8,128)(2,1)}, bf16[2,256,256]{2,1,0:T(8,128)(2,1)}, u32[]{:S(2)}, u32[]{:S(2)}) collective-permute-start(bf16[2,256,256]{2,1,0:T(8,128)(2,1)} %collective-permute-done.4), channel_id=1, source_target_pairs={{0,4},{4,8},{8,12},{1,5},{5,9},{9,13},{2,6},{6,10},{10,14},{3,7},{... | collective-permute-start | bytes 786440 | tf_op jit(solution)/shard_map/ppermute | solution.py:41
  135.3 10.9 %collective-permute-start.6 = (bf16[2,256,256]{2,1,0:T(8,128)(2,1)}, bf16[2,256,256]{2,1,0:T(8,128)(2,1)S(1)}, u32[]{:S(2)}, u32[]{:S(2)}) collective-permute-start(bf16[2,256,256]{2,1,0:T(8,128)(2,1)} %collective-permute-done.5), channel_id=1, source_target_pairs={{0,4},{4,8},{8,12},{1,5},{5,9},{9,13},{2,6},{6,10},{10,14},{3,7},{... | collective-permute-start | bytes 786440 | tf_op jit(solution)/shard_map/ppermute | solution.py:41
  146.2 2.1 fusion.11
  154.0 6.0 %convolution_convert_fusion.3 = bf16[256,2048]{1,0:T(8,128)(2,1)} fusion(bf16[256,1344]{0,1:T(8,128)(2,1)S(1)} %copy-done, bf16[2048,1344]{0,1:T(8,128)(2,1)} %all-gather.15.cloned.1.call-done), kind=kOutput, calls=%fused_computation.25 | convolution fusion | flops 1409810432 | bytes 7241728 | tf_op jit(solution)/shard_map/td,hd->th/dot_general | solution.py:147
  161.9 2.4 fusion.52
  164.4 2.5 reshape_squeeze.9
  166.9 2.5 reshape_squeeze.10
  169.4 2.9 copy.117
  172.3 18.4 %all-gather.11.cloned.1.call-done = bf16[5376,512]{1,0:T(8,128)(2,1)} async-done(((bf16[1344,512]{1,0:T(8,128)(2,1)}), bf16[5376,512]{1,0:T(8,128)(2,1)}) %all-gather.11.cloned.1.call-update) | async-done | bytes 5505040 | tf_op jit(solution)/shard_map/all_gather | solution.py:87
  190.8 5.0 fusion.55
  198.6 22.1 %reduce-scatter.7.cloned.1.call-done = bf16[256,512]{1,0:T(8,128)(2,1)} async-done(((bf16[256,2048]{1,0:T(8,128)(2,1)}), bf16[256,512]{1,0:T(8,128)(2,1)}) %reduce-scatter.7.cloned.1.call-update) | async-done | bytes 262160 | tf_op jit(solution)/shard_map/reduce_scatter | solution.py:153
  221.8 3.2 fusion.19
  225.0 7.2 %fusion.2 = (f32[2,2,256]{2,1,0:T(2,128)S(1)}, f32[2,2,256,1280]{2,3,1,0:T(8,128)}) fusion(f32[2,1280,256,2]{2,1,3,0:T(8,128)} %fusion.19, bf16[1280,2,128,1]{0,2,3,1:T(8,128)(2,1)S(1)} %copy-done.14, pred[256,1280]{0,1:T(8,128)(4,1)S(1)} %copy-done.36, bf16[256,2,2,64]{3,0,2,1:T(8,128)(2,1)S(1)} %bitcast.114, bf16[256,2,2,64]{3,0,2,1:T(8,128)(2,1)S(1)} %bitcast.116), kind=kOutput, calls=%fused_computation.9 | convolution fusion | flops 342623488 | bytes 11735040 | tf_op jit(solution)/shard_map/div | solution.py:133
  232.2 3.8 fusion.14
  236.8 25.9 %all-gather.13.cloned.1.call-done = bf16[256,2048]{0,1:T(8,128)(2,1)} async-done(((bf16[256,512]{0,1:T(8,128)(2,1)}), bf16[256,2048]{0,1:T(8,128)(2,1)}) %all-gather.13.cloned.1.call-update) | async-done | bytes 1048592 | tf_op jit(solution)/shard_map/all_gather | solution.py:139
  262.7 5.2 %convolution_convert_fusion.1 = bf16[2048,1344]{0,1:T(8,128)(2,1)} fusion(bf16[256,2048]{0,1:T(8,128)(2,1)} %all-gather.13.cloned.1.call-done, bf16[256,1344]{0,1:T(8,128)(2,1)S(1)} %copy-done), kind=kOutput, calls=%fused_computation.6 | convolution fusion | flops 1412038656 | bytes 7241728 | tf_op jit(solution)/shard_map/th,td->hd/dot_general | solution.py:159
  268.3 5.7 %fusion.4 = bf16[2,2,256,1280]{2,3,1,0:T(8,128)(2,1)S(1)} fusion(f32[2,1280,256,2]{2,1,3,0:T(8,128)} %fusion.19, f32[2,2,256,1280]{2,3,1,0:T(8,128)} %get-tuple-element.51, f32[2,2,256]{2,1,0:T(2,128)S(1)} %get-tuple-element.50), kind=kLoop, calls=%fused_computation.11 | loop fusion | flops 5242880 | bytes 13111296 | tf_op jit(solution)/shard_map/convert_element_type | solution.py:174
  275.1 3.5 fusion.7
  280.0 2.1 collective-permute-done.7
  286.8 8.9 %collective-permute-done.8 = bf16[2,256,256]{1,2,0:T(8,128)(2,1)} collective-permute-done((bf16[2,256,256]{1,2,0:T(8,128)(2,1)}, bf16[2,256,256]{1,2,0:T(8,128)(2,1)}, u32[]{:S(2)}, u32[]{:S(2)}) %collective-permute-start.8) | collective-permute-done | bytes 262176 | tf_op jit(solution)/shard_map/ppermute | solution.py:41
  300.7 5.0 collective-permute-done.9
  309.0 2.0 fusion.21
  311.8 3.4 collective-permute-done.10
  318.8 7.7 %fusion = bf16[5376,1024]{0,1:T(8,128)(2,1)} fusion(bf16[256,5376]{0,1:T(8,128)(2,1)} %all-gather.7.cloned.1.call-done, bf16[256,256]{1,0:T(8,128)(2,1)S(1)} %copy.109, bf16[256,256]{1,0:T(8,128)(2,1)S(1)} %copy.108, bf16[256,512]{1,0:T(8,128)(2,1)S(1)} %bitcast.113), kind=kOutput, calls=%fused_computation.2 | convolution fusion | flops 2825650176 | bytes 14286848 | tf_op jit(solution)/shard_map/td,tc->dc/dot_general | solution.py:230
  326.5 14.7 %copy.133 = bf16[5376,1024]{1,0:T(8,128)(2,1)} copy(bf16[5376,1024]{0,1:T(8,128)(2,1)} %fusion) | data formatting | bytes 22020096
  342.2 4.5 fusion.49
  346.7 3.3 convolution_add_fusion.1
  349.9 6.0 %fusion.1 = bf16[256,5376]{0,1:T(8,128)(2,1)} fusion(f32[256,5376]{0,1:T(8,128)} %convolution_add_fusion.1, bf16[5376,256]{1,0:T(8,128)(2,1)} %all-gather.17.cloned.1.call-done, f32[2,256,256]{1,2,0:T(8,128)S(1)} %copy-done.13), kind=kOutput, calls=%fused_computation.5 | convolution fusion | flops 707395584 | bytes 11141120 | tf_op jit(solution)/shard_map/tc,dc->td/dot_general | solution.py:221
  357.1 5.6 %convolution_convert_fusion.2 = bf16[256,1344]{0,1:T(8,128)(2,1)} fusion(bf16[2048,1344]{0,1:T(8,128)(2,1)} %all-gather.15.cloned.1.call-done, bf16[256,2048]{0,1:T(8,128)(2,1)S(1)} %copy-done.26), kind=kOutput, calls=%fused_computation.24 | convolution fusion | flops 1409630208 | bytes 7241728 | tf_op jit(solution)/shard_map/dot_general | solution.py:141
  362.7 3.7 convert_element_type.115
  366.4 74.7 %reduce-scatter.13.cloned.1.call-done = bf16[1344,1024]{1,0:T(8,128)(2,1)} async-done(((bf16[5376,1024]{1,0:T(8,128)(2,1)}), bf16[1344,1024]{1,0:T(8,128)(2,1)}) %reduce-scatter.13.cloned.1.call-update) | async-done | bytes 2752528
  441.1 4.5 copy.134
  445.6 3.2 slice.84
  448.8 3.8 copy.110
  452.6 2.6 fusion.51
  455.2 2.9 copy.111
  459.6 38.4 %reduce-scatter.9.cloned.1.call-done = bf16[256,1344]{0,1:T(8,128)(2,1)} async-done(((bf16[256,5376]{0,1:T(8,128)(2,1)}), bf16[256,1344]{0,1:T(8,128)(2,1)}) %reduce-scatter.9.cloned.1.call-update) | async-done | bytes 688144 | tf_op jit(solution)/shard_map/reduce_scatter | solution.py:224
  (171 shorter events, 49.5 us)
Async XLA Ops:
  7.2 146.9 %copy-start = (bf16[256,1344]{0,1:T(8,128)(2,1)S(1)}, bf16[256,1344]{0,1:T(8,128)(2,1)}, u32[]{:S(2)}) copy-start(bf16[256,1344]{0,1:T(8,128)(2,1)} %param.17) | copy-start | bytes 2064388
  7.2 21.2 %copy-start.38 = (s32[1024]{0:T(1024)S(1)}, s32[1024]{0:T(1024)}, u32[]{:S(2)}) copy-start(s32[1024]{0:T(1024)} %param.16) | copy-start | bytes 12292
  7.2 62.1 %all-gather.7.cloned.1.call-start = ((), (), s32[]{:S(2)}) async-start(), calls=%async_computation.4 | async-start | bytes 3440640 | tf_op jit(solution)/shard_map/all_gather | solution.py:85
  7.9 88.0 %all-gather.9.cloned.1.call-start = ((), (), s32[]{:S(2)}) async-start(), calls=%async_computation.5 | async-start | bytes 3440640 | tf_op jit(solution)/shard_map/all_gather | solution.py:88
  8.7 145.3 %all-gather.15.cloned.1.call-start = ((), (), s32[]{:S(2)}) async-start(), calls=%async_computation.8 | async-start | bytes 6881280 | tf_op jit(solution)/shard_map/all_gather | solution.py:143
  9.4 181.3 %all-gather.11.cloned.1.call-start = ((), (), s32[]{:S(2)}) async-start(), calls=%async_computation.6 | async-start | bytes 6881280 | tf_op jit(solution)/shard_map/all_gather | solution.py:87
  10.0 210.7 %reduce-scatter.7.cloned.1.call-start = ((), (), s32[]{:S(2)}) async-start(), calls=%async_computation.9 | async-start | bytes 1310720 | tf_op jit(solution)/shard_map/reduce_scatter | solution.py:153
  10.1 15.8 %collective-permute-start = (bf16[1344,256]{1,0:T(8,128)(2,1)S(1)}, bf16[1344,256]{1,0:T(8,128)(2,1)S(1)}, u32[]{:S(2)}, u32[]{:S(2)}) collective-permute-start(bf16[1344,256]{1,0:T(8,128)(2,1)S(1)} %copy-done.11), channel_id=1, source_target_pairs={{0,4},{4,8},{8,12},{12,0},{1,5},{5,9},{9,13},{13,1},{2,6},{6,10},{... | collective-permute-start | bytes 2064392 | tf_op jit(solution)/shard_map/ppermute | solution.py:29
  10.6 19.3 %collective-permute-start.2 = (bf16[1344,256]{1,0:T(8,128)(2,1)S(1)}, bf16[1344,256]{1,0:T(8,128)(2,1)S(1)}, u32[]{:S(2)}, u32[]{:S(2)}) collective-permute-start(bf16[1344,256]{1,0:T(8,128)(2,1)S(1)} %copy-done.11), channel_id=1, source_target_pairs={{4,0},{8,4},{12,8},{0,12},{5,1},{9,5},{13,9},{1,13},{6,2},{10,6},{... | collective-permute-start | bytes 2064392 | tf_op jit(solution)/shard_map/ppermute | solution.py:31
  25.8 10.5 %copy-start.31 = (bf16[1344,256]{1,0:T(8,128)(2,1)}, bf16[1344,256]{1,0:T(8,128)(2,1)S(1)}, u32[]{:S(2)}) copy-start(bf16[1344,256]{1,0:T(8,128)(2,1)S(1)} %collective-permute-done) | copy-start | bytes 2064388
  25.8 10.5 %collective-permute-start.1 = (bf16[1344,256]{1,0:T(8,128)(2,1)S(1)}, bf16[1344,256]{1,0:T(8,128)(2,1)}, u32[]{:S(2)}, u32[]{:S(2)}) collective-permute-start(bf16[1344,256]{1,0:T(8,128)(2,1)S(1)} %collective-permute-done), channel_id=1, source_target_pairs={{0,4},{4,8},{8,12},{12,0},{1,5},{5,9},{9,13},{13,1},{2,6},{6,10},{... | collective-permute-start | bytes 2064392 | tf_op jit(solution)/shard_map/ppermute | solution.py:29
  29.0 7.3 %copy-start.19 = (f32[256,64]{1,0:T(8,128)}, f32[256,64]{1,0:T(8,128)S(1)}, u32[]{:S(2)}) copy-start(f32[256,64]{1,0:T(8,128)S(1)} %get-tuple-element.46) | copy-start | bytes 196612
  29.0 7.3 %copy-start.21 = (f32[256,64]{1,0:T(8,128)}, f32[256,64]{1,0:T(8,128)S(1)}, u32[]{:S(2)}) copy-start(f32[256,64]{1,0:T(8,128)S(1)} %get-tuple-element.47) | copy-start | bytes 196612
  29.8 6.5 %copy-start.32 = (bf16[1344,256]{1,0:T(8,128)(2,1)}, bf16[1344,256]{1,0:T(8,128)(2,1)S(1)}, u32[]{:S(2)}) copy-start(bf16[1344,256]{1,0:T(8,128)(2,1)S(1)} %collective-permute-done.2) | copy-start | bytes 2064388
  40.5 60.0 %copy-start.40 = (f32[128]{0:T(128)S(1)}, f32[128]{0:T(128)}, u32[]{:S(2)}) copy-start(f32[128]{0:T(128)} %param.15) | copy-start | bytes 1540
  69.3 33.6 %copy-start.2 = (bf16[256,5376]{0,1:T(8,128)(2,1)S(1)}, bf16[256,5376]{0,1:T(8,128)(2,1)}, u32[]{:S(2)}) copy-start(bf16[256,5376]{0,1:T(8,128)(2,1)} %all-gather.7.cloned.1.call-done) | copy-start | bytes 8257540
  96.0 4.6 copy-start.33
  103.0 3.3 copy-start.29
  106.9 3.3 collective-permute-start.3
  110.9 10.9 %collective-permute-start.4 = (bf16[2,256,256]{2,1,0:T(8,128)(2,1)S(1)}, bf16[2,256,256]{2,1,0:T(8,128)(2,1)}, u32[]{:S(2)}, u32[]{:S(2)}) collective-permute-start(bf16[2,256,256]{2,1,0:T(8,128)(2,1)S(1)} %collective-permute-done.3), channel_id=1, source_target_pairs={{0,4},{4,8},{8,12},{1,5},{5,9},{9,13},{2,6},{6,10},{10,14},{3,7},{... | collective-permute-start | bytes 786440 | tf_op jit(solution)/shard_map/ppermute | solution.py:41
  121.8 13.5 %collective-permute-start.5 = (bf16[2,256,256]{2,1,0:T(8,128)(2,1)}, bf16[2,256,256]{2,1,0:T(8,128)(2,1)}, u32[]{:S(2)}, u32[]{:S(2)}) collective-permute-start(bf16[2,256,256]{2,1,0:T(8,128)(2,1)} %collective-permute-done.4), channel_id=1, source_target_pairs={{0,4},{4,8},{8,12},{1,5},{5,9},{9,13},{2,6},{6,10},{10,14},{3,7},{... | collective-permute-start | bytes 786440 | tf_op jit(solution)/shard_map/ppermute | solution.py:41
  135.3 13.0 %collective-permute-start.6 = (bf16[2,256,256]{2,1,0:T(8,128)(2,1)}, bf16[2,256,256]{2,1,0:T(8,128)(2,1)S(1)}, u32[]{:S(2)}, u32[]{:S(2)}) collective-permute-start(bf16[2,256,256]{2,1,0:T(8,128)(2,1)} %collective-permute-done.5), channel_id=1, source_target_pairs={{0,4},{4,8},{8,12},{1,5},{5,9},{9,13},{2,6},{6,10},{10,14},{3,7},{... | collective-permute-start | bytes 786440 | tf_op jit(solution)/shard_map/ppermute | solution.py:41
  160.0 102.7 %all-gather.13.cloned.1.call-start = ((), (), s32[]{:S(2)}) async-start(), calls=%async_computation.7 | async-start | bytes 1310720 | tf_op jit(solution)/shard_map/all_gather | solution.py:139
  172.3 25.3 %copy-start.39 = (f32[128]{0:T(128)S(1)}, f32[128]{0:T(128)}, u32[]{:S(2)}) copy-start(f32[128]{0:T(128)} %param.14) | copy-start | bytes 1540
  197.0 24.8 %copy-start.3 = (f32[256,4,128]{2,1,0:T(4,128)}, f32[256,4,128]{2,1,0:T(4,128)S(1)}, u32[]{:S(2)}) copy-start(f32[256,4,128]{2,1,0:T(4,128)S(1)} %reshape.277) | copy-start | bytes 1572868
  197.0 24.8 %copy-start.6 = (bf16[1280,2,128]{2,1,0:T(2,128)(2,1)S(1)}, bf16[1280,2,128]{2,1,0:T(2,128)(2,1)}, u32[]{:S(2)}) copy-start(bf16[1280,2,128]{2,1,0:T(2,128)(2,1)} %reshape_squeeze.9) | copy-start | bytes 1966084
  197.6 24.2 %copy-start.27 = (f32[256,4]{1,0:T(8,128)}, f32[256,4]{1,0:T(8,128)S(1)}, u32[]{:S(2)}) copy-start(f32[256,4]{1,0:T(8,128)S(1)} %copy.90) | copy-start | bytes 12292
  221.8 3.2 copy-start.17
  236.0 113.9 %all-gather.17.cloned.1.call-start = ((), (), s32[]{:S(2)}) async-start(), calls=%async_computation.10 | async-start | bytes 3440640 | tf_op jit(solution)/shard_map/all_gather | solution.py:215
  236.7 126.0 %reduce-scatter.11.cloned.1.call-start = ((), (), s32[]{:S(2)}) async-start(), calls=%async_computation.12 | async-start | bytes 6881280 | tf_op jit(solution)/shard_map/reduce_scatter | solution.py:158
  268.0 173.1 %reduce-scatter.13.cloned.1.call-start = ((), (), s32[]{:S(2)}) async-start(), calls=%async_computation.13 | async-start | bytes 13762560
  278.6 5.7 %copy-start.15 = (bf16[1280,2,128,1]{0,2,3,1:T(8,128)(2,1)S(1)}, bf16[1280,2,128,1]{0,2,3,1:T(8,128)(2,1)}, u32[]{:S(2)}) copy-start(bf16[1280,2,128,1]{0,2,3,1:T(8,128)(2,1)} %copy.117) | copy-start | bytes 1966084
  278.6 3.6 collective-permute-start.7
  282.9 12.8 %collective-permute-start.8 = (bf16[2,256,256]{1,2,0:T(8,128)(2,1)}, bf16[2,256,256]{1,2,0:T(8,128)(2,1)}, u32[]{:S(2)}, u32[]{:S(2)}) collective-permute-start(bf16[2,256,256]{1,2,0:T(8,128)(2,1)} %fusion.29), channel_id=1, source_target_pairs={{4,0},{8,4},{12,8},{5,1},{9,5},{13,9},{6,2},{10,6},{14,10},{7,3},{... | collective-permute-start | bytes 786440 | tf_op jit(solution)/shard_map/ppermute | solution.py:41
  284.8 13.9 %copy-start.23 = (f32[256,64]{1,0:T(8,128)S(1)}, f32[256,64]{1,0:T(8,128)}, u32[]{:S(2)}) copy-start(f32[256,64]{1,0:T(8,128)} %copy-done.21) | copy-start | bytes 196612
  286.8 11.9 %copy-start.24 = (f32[256,4,64]{2,1,0:T(4,128)S(1)}, f32[256,4,64]{2,1,0:T(4,128)}, u32[]{:S(2)}) copy-start(f32[256,4,64]{2,1,0:T(4,128)} %copy.136) | copy-start | bytes 786436
  286.8 11.9 %copy-start.25 = (f32[256,4,64]{2,1,0:T(4,128)S(1)}, f32[256,4,64]{2,1,0:T(4,128)}, u32[]{:S(2)}) copy-start(f32[256,4,64]{2,1,0:T(4,128)} %copy.135) | copy-start | bytes 786436
  286.8 13.2 %copy-start.4 = (f32[256,4,128]{2,1,0:T(4,128)S(1)}, f32[256,4,128]{2,1,0:T(4,128)}, u32[]{:S(2)}) copy-start(f32[256,4,128]{2,1,0:T(4,128)} %copy-done.3) | copy-start | bytes 1572868
  297.4 8.4 %collective-permute-start.9 = (bf16[2,256,256]{1,2,0:T(8,128)(2,1)}, bf16[2,256,256]{1,2,0:T(8,128)(2,1)}, u32[]{:S(2)}, u32[]{:S(2)}) collective-permute-start(bf16[2,256,256]{1,2,0:T(8,128)(2,1)} %fusion.32), channel_id=1, source_target_pairs={{4,0},{8,4},{12,8},{5,1},{9,5},{13,9},{6,2},{10,6},{14,10},{7,3},{... | collective-permute-start | bytes 786440 | tf_op jit(solution)/shard_map/ppermute | solution.py:41
  299.1 9.9 %copy-start.28 = (f32[256,4]{1,0:T(8,128)S(1)}, f32[256,4]{1,0:T(8,128)}, u32[]{:S(2)}) copy-start(f32[256,4]{1,0:T(8,128)} %copy-done.27) | copy-start | bytes 12292
  307.5 7.6 %collective-permute-start.10 = (bf16[2,256,256]{1,2,0:T(8,128)(2,1)}, bf16[2,256,256]{1,2,0:T(8,128)(2,1)}, u32[]{:S(2)}, u32[]{:S(2)}) collective-permute-start(bf16[2,256,256]{1,2,0:T(8,128)(2,1)} %fusion.24), channel_id=1, source_target_pairs={{4,0},{8,4},{12,8},{5,1},{9,5},{13,9},{6,2},{10,6},{14,10},{7,3},{... | collective-permute-start | bytes 786440 | tf_op jit(solution)/shard_map/ppermute | solution.py:41
  311.0 5.2 %copy-start.9 = (bf16[256,4,128]{2,1,0:T(4,128)(2,1)}, bf16[256,4,128]{2,1,0:T(4,128)(2,1)S(1)}, u32[]{:S(2)}) copy-start(bf16[256,4,128]{2,1,0:T(4,128)(2,1)S(1)} %fusion.21) | copy-start | bytes 786436
  311.0 5.4 %copy-start.34 = (f32[256,64]{0,1:T(8,128)S(1)}, f32[256,64]{0,1:T(8,128)}, u32[]{:S(2)}) copy-start(f32[256,64]{0,1:T(8,128)} %copy.86) | copy-start | bytes 196612
  316.2 10.3 %copy-start.12 = (f32[2,256,256]{1,2,0:T(8,128)}, f32[2,256,256]{1,2,0:T(8,128)S(1)}, u32[]{:S(2)}) copy-start(f32[2,256,256]{1,2,0:T(8,128)S(1)} %fusion.33) | copy-start | bytes 1572868
  341.3 156.8 %reduce-scatter.9.cloned.1.call-start = ((), (), s32[]{:S(2)}) async-start(), calls=%async_computation.11 | async-start | bytes 3440640 | tf_op jit(solution)/shard_map/reduce_scatter | solution.py:224
  342.2 4.5 copy-start.5
  346.7 3.3 copy-start.13
  455.2 42.8 %copy-start.1 = (bf16[256,1344]{0,1:T(8,128)(2,1)S(1)}, bf16[256,1344]{0,1:T(8,128)(2,1)}, u32[]{:S(2)}) copy-start(bf16[256,1344]{0,1:T(8,128)(2,1)} %param.17) | copy-start | bytes 2064388
  (14 other events, 23.4 us)
Sparse Core Ops, SparseCore 0:
  9.6 59.6 all-gather.6
  70.9 25.0 all-gather.8
  97.5 46.0 all-gather.14
  145.0 45.7 all-gather.10
  193.5 27.1 reduce-scatter.6
  236.1 26.5 all-gather.12
  264.4 28.5 all-gather.16
  295.7 55.3 reduce-scatter.10
  353.6 87.4 reduce-scatter.12
  443.8 54.1 reduce-scatter.8
